TPU v7x, 512 devices: a whole 4x4x16 slice. The times are simulated.
512 devices in a mesh: row: 16 (over z), col: 32 (over y, x, core).
Axes of the slice: x: 4, y: 4, z: 16, core: 2. Of those that a mesh axis runs over, the one named last changes fastest.
Arguments:
- centroids: float32 [3, 32768], P(None, ('col', 'row')), may hold values from 0 to 1, as said below
- areas: float32 [32768], P(('col', 'row')), may hold values from 0.5 to 2
- conductance: float32 [32768], P(('col', 'row')), may hold values from 0.1 to 1
- power: float32 [16, 32768], P(None, ('col', 'row')), may hold values from -3 to 6
Outputs:
- solution: float32 [16, 32768], P(None, ('col', 'row'))
- residual: float32 [16, 32768], P(None, ('col', 'row'))
Inputs may be any that keep to these rules, and one draw needn't show every extreme that they name: `centroids`: panels lie on 16 parallel fins across the unit cube.
All inputs are finite; a program needn't handle non-finite values.
Results may differ from a plain program's by a relative error of at most 0.00039.
Values may be sent and summed in bfloat16 or wider, within the bound.
No kernel may reach another device: no remote copies, remote signals or barrier semaphores. Data moves between devices by JAX's collectives and lax.ppermute only.
A program may use at most 64 MiB of HBM per device.

v0:
```python
import math
import jax
import jax.numpy as jnp
from jax import lax
from jax.sharding import PartitionSpec as P


def kernel_tile(src, tgt, scale, delta2):
    dx = src[0][:, None] - tgt[0][None, :]
    dy = src[1][:, None] - tgt[1][None, :]
    dz = src[2][:, None] - tgt[2][None, :]
    dist2 = dx * dx + dy * dy + dz * dz
    return (src[3][:, None] * scale * lax.rsqrt(dist2 + delta2)).astype(jnp.bfloat16)


def inner(left, right):
    return jnp.dot(left, right.T, precision=lax.Precision.HIGHEST)


def lower_inverse(gram):
    factor = jnp.linalg.cholesky(gram)
    eye = jnp.eye(gram.shape[0], dtype=jnp.float32)
    return (factor, jax.scipy.linalg.solve_triangular(factor, eye, lower=True))


def reduce_small(terms):
    return lax.psum(terms, ("row", "col"))


def body(centroids, areas, conductance, power):
    high = lax.Precision.HIGHEST
    width = power.shape[1]
    nrhs = power.shape[0]
    panels = width * lax.axis_size("row") * lax.axis_size("col")
    scale = 4.0 / (math.pi * panels)
    delta2 = 16.0 / panels
    geom = jnp.concatenate([centroids, areas[None, :]], 0)
    sources = lax.all_gather(geom, "col", axis=1, tiled=True)
    targets = lax.all_gather(centroids, "row", axis=1, tiled=True)
    tgt_len = targets.shape[1]
    rhs, cond_row = (power, conductance[None, :])
    factor0, inverse0 = lower_inverse(reduce_small(inner(rhs, rhs)))
    basis = [jnp.dot(inverse0, rhs, precision=high)]
    blocks = {}
    for step in range(2):
        field = basis[step]
        empty = jnp.zeros((nrhs, tgt_len), jnp.float32)
        piece = lax.all_gather(field.astype(jnp.bfloat16), "col", axis=1, tiled=True)
        cols = piece.shape[1]
        step_len = width * max(1, 512 // width)
        turns = cols // step_len

        def one(turn, acc):
            vec = lax.dynamic_slice_in_dim(piece, turn * step_len, step_len, 1)
            src = lax.dynamic_slice_in_dim(sources, turn * step_len, step_len, 1)
            tile = kernel_tile(src, targets, scale, delta2)
            return acc + jnp.dot(vec, tile, preferred_element_type=jnp.float32)

        apply_total = lax.fori_loop(0, turns, one, empty)
        product = lax.psum_scatter(apply_total, "row", scatter_dimension=1, tiled=True)
        image = cond_row * field + product
        coeffs = list(reduce_small(tuple((inner(vec, image) for vec in basis))))
        for idx in range(step + 1):
            image = image - jnp.dot(coeffs[idx].T, basis[idx], precision=high)
        gram = reduce_small(inner(image, image))
        for idx in range(step + 1):
            blocks[idx, step] = coeffs[idx]
        factor, inverse = lower_inverse(gram)
        blocks[step + 1, step] = factor.T
        basis.append(jnp.dot(inverse, image, precision=high))
    hbar = jnp.zeros((3 * nrhs, 2 * nrhs), jnp.float32)
    for key in blocks:
        hbar = hbar.at[
            key[0] * nrhs : (key[0] + 1) * nrhs, key[1] * nrhs : (key[1] + 1) * nrhs
        ].set(blocks[key])
    target = jnp.zeros((3 * nrhs, nrhs), jnp.float32).at[:nrhs].set(factor0.T)
    normal = jnp.dot(hbar.T, hbar, precision=high)
    chol = jnp.linalg.cholesky(normal)
    coeff_y = jax.scipy.linalg.cho_solve((chol, True), jnp.dot(hbar.T, target, precision=high))
    coeff_z = target - jnp.dot(hbar, coeff_y, precision=high)
    solution = jnp.dot(coeff_y[:nrhs].T, basis[0], precision=high) + jnp.dot(
        coeff_y[nrhs:].T, basis[1], precision=high
    )
    residual = jnp.dot(coeff_z[:nrhs].T, basis[0], precision=high) + jnp.dot(
        coeff_z[nrhs : 2 * nrhs].T, basis[1], precision=high
    )
    residual = residual + jnp.dot(coeff_z[2 * nrhs :].T, basis[2], precision=high)
    return (solution, residual)


def solution(mesh):
    return jax.shard_map(
        body,
        mesh=mesh,
        in_specs=(
            P(None, ("col", "row")),
            P(("col", "row")),
            P(("col", "row")),
            P(None, ("col", "row")),
        ),
        out_specs=(P(None, ("col", "row")), P(None, ("col", "row"))),
        check_vma=False,
    )
```

profile of v0, /device:TPU:1, one launch (start us, length us, event | category | flops | bytes accessed | tf_op | source)
XLA Modules:
  0.0 797.1 jit_solution(8880030113008817273)
XLA Ops:
  8.0 111.0 %psum.42 = f32[16,16]{0,1:T(8,128)S(1)} all-reduce(f32[16,16]{0,1:T(8,128)S(1)} %fusion.59), channel_id=1, replica_groups=mesh['row'=16,'col'=32] {'row','col'}, use_global_device_ids=true, to_apply=%region_0.0 | all-reduce | flops 256 | bytes 2048 | tf_op jit(solution)/shard_map/psum | solution.py:27
  119.1 1.5 cholesky.94
  121.9 1.2 custom-call.20
  123.5 22.9 %all-gather = bf16[32,64,16]{1,2,0:T(8,128)(2,1)S(1)} all-gather(bf16[1,64,16]{1,2,0:T(8,128)(2,1)S(1)} %convert_bitcast_fusion.1), channel_id=1, replica_groups=mesh['row'=16,'col'=32] {'col'}, dimensions={0}, use_global_device_ids=true | all-gather | bytes 67584 | tf_op jit(solution)/shard_map/all_gather | solution.py:48
  146.7 23.6 %all-gather.1 = f32[32,64,4]{1,2,0:T(4,128)S(1)} all-gather(f32[1,64,4]{1,2,0:T(4,128)S(1)} %maximum_bitcast_fusion), channel_id=1, replica_groups=mesh['row'=16,'col'=32] {'col'}, dimensions={0}, use_global_device_ids=true | all-gather | bytes 33792 | tf_op jit(solution)/shard_map/all_gather | solution.py:38
  170.4 19.9 %all-gather.2 = f32[16,64,3]{1,2,0:T(4,128)S(1)} all-gather(f32[1,64,3]{1,2,0:T(4,128)S(1)} %bitcast.175), channel_id=1, replica_groups=mesh['row'=16,'col'=32] {'row'}, dimensions={0}, use_global_device_ids=true | all-gather | bytes 13056 | tf_op jit(solution)/shard_map/all_gather | solution.py:39
  190.4 4.5 while.34
  191.6 1.0 convolution_add_fusion.7
  196.0 59.8 %reduce-scatter.7.cloned.1.call-done = f32[64,16]{1,0:T(8,128)} async-done(((f32[1024,16]{1,0:T(8,128)}), f32[64,16]{1,0:T(8,128)}) %reduce-scatter.7.cloned.1.call-update) | async-done | bytes 4112
  256.7 111.7 %psum.43 = f32[16,16]{1,0:T(8,128)S(1)} all-reduce(f32[16,16]{1,0:T(8,128)S(1)} %fusion.46), channel_id=1, replica_groups=mesh['row'=16,'col'=32] {'row','col'}, use_global_device_ids=true, to_apply=%region_6.0 | all-reduce | flops 256 | bytes 2048 | tf_op jit(solution)/shard_map/psum | solution.py:27
  368.7 100.0 %psum.44 = f32[16,16]{0,1:T(8,128)S(1)} all-reduce(f32[16,16]{0,1:T(8,128)S(1)} %fusion.61), channel_id=1, replica_groups=mesh['row'=16,'col'=32] {'row','col'}, use_global_device_ids=true, to_apply=%region_7.0 | all-reduce | flops 256 | bytes 2048 | tf_op jit(solution)/shard_map/psum | solution.py:27
  468.8 1.5 cholesky.105
  471.6 1.2 custom-call.21
  473.2 24.4 %all-gather.3 = bf16[32,64,16]{1,2,0:T(8,128)(2,1)S(1)} all-gather(bf16[1,64,16]{1,2,0:T(8,128)(2,1)S(1)} %convert_bitcast_fusion), channel_id=1, replica_groups=mesh['row'=16,'col'=32] {'col'}, dimensions={0}, use_global_device_ids=true | all-gather | bytes 67584 | tf_op jit(solution)/shard_map/all_gather | solution.py:48
  497.7 4.5 while.35
  505.2 51.2 %reduce-scatter.9.cloned.1.call-done = f32[64,16]{1,0:T(8,128)} async-done(((f32[1024,16]{1,0:T(8,128)}), f32[64,16]{1,0:T(8,128)}) %reduce-scatter.9.cloned.1.call-update) | async-done | bytes 4112
  557.5 111.9 %all-reduce.2 = (f32[16,16]{1,0:T(8,128)S(1)}, f32[16,16]{1,0:T(8,128)S(1)}) all-reduce(f32[16,16]{1,0:T(8,128)S(1)} %fusion.54, f32[16,16]{1,0:T(8,128)S(1)} %fusion.53), channel_id=1, replica_groups=mesh['row'=16,'col'=32] {'row','col'}, use_global_device_ids=true, to_apply=%region_12.0 | all-reduce | flops 512 | bytes 4096 | tf_op jit(solution)/shard_map/psum | solution.py:27
  669.9 100.3 %psum.47 = f32[16,16]{0,1:T(8,128)S(1)} all-reduce(f32[16,16]{0,1:T(8,128)S(1)} %fusion.63), channel_id=1, replica_groups=mesh['row'=16,'col'=32] {'row','col'}, use_global_device_ids=true, to_apply=%region_14.0 | all-reduce | flops 256 | bytes 2048 | tf_op jit(solution)/shard_map/psum | solution.py:27
  770.3 1.5 cholesky.116
  773.3 2.0 dynamic-slice_select_fusion
  775.3 2.1 scatter.24
  779.3 2.9 cholesky.41
  783.5 2.4 custom-call.15
  786.7 1.2 custom-call.22
  (108 shorter events, 27.4 us)
Async XLA Ops:
  7.2 0.7 copy-start
  7.2 139.5 %copy-start.3 = (f32[64]{0:T(128)S(1)}, f32[64]{0:T(128)}, u32[]{:S(2)}) copy-start(f32[64]{0:T(128)} %param.24) | copy-start | bytes 772
  7.2 139.5 %copy-start.2 = (f32[3,64]{1,0:T(4,128)S(1)}, f32[3,64]{1,0:T(4,128)}, u32[]{:S(2)}) copy-start(f32[3,64]{1,0:T(4,128)} %param.23) | copy-start | bytes 2308
  7.2 248.6 %reduce-scatter.7.cloned.1.call-start = ((), (), s32[]{:S(2)}) async-start(), calls=%async_computation.2 | async-start | bytes 557056
  194.9 61.7 %copy-start.1 = (f32[64]{0:T(128)S(1)}, f32[64]{0:T(128)}, u32[]{:S(2)}) copy-start(f32[64]{0:T(128)} %param.25) | copy-start | bytes 772
  195.9 360.5 %reduce-scatter.9.cloned.1.call-start = ((), (), s32[]{:S(2)}) async-start(), calls=%async_computation.3 | async-start | bytes 557056
  502.3 1.6 copy-start.4
Sparse Core Ops, SparseCore 0:
  196.0 59.6 reduce-scatter.6
  503.4 52.9 reduce-scatter.8
where the time goes:
time: 798 us; the launch traced here: 797 us
  blocking collectives  626 us (78%)
  waiting for transfers between devices  111 us (14%)
  other arithmetic  22.3 us (3%)
  between operations  14.2 us (2%)
  matrix products  13.4 us (2%)
  local copies, waits for them, and re-layouts  10.1 us (1%)
    psum x5, blocking collectives, reduce_small(): return lax.psum(terms, ('row', 'col'))  535 us
    unnamed x4, waiting for transfers between devices  111 us
    all_gather x2, blocking collectives, body(): lax.all_gather(field.astype(jnp.bfloat16), 'col', axis=1, tiled=True)  47.3 us
    all_gather x1, blocking collectives, body(): sources = lax.all_gather(geom, 'col', axis=1, tiled=True)  23.6 us
    all_gather x1, blocking collectives, body(): targets = lax.all_gather(centroids, 'row', axis=1, tiled=True)  19.9 us
  transfers between devices with their start and end apart: 2, of which 2 were waited for; matrix products, arithmetic and copies ran while one was open for 0% of the time, Pallas kernels for 0%

commit v1 on v0

--- a/solution.py
+++ b/solution.py
@@ -24,7 +24,7 @@
 
 
 def reduce_small(terms):
-    return lax.psum(terms, ("row", "col"))
+    return lax.psum(lax.psum(terms, "col"), "row")
 
 
 def body(centroids, areas, conductance, power):

time: 798 us -> 842 us (1.055)
  blocking collectives: 626 us -> 663 us
    psum x5 -> x10, blocking collectives: 535 us -> 557 us  [reduce_small(): return lax.psum(lax.psum(terms, 'col'), 'row')]
    all_gather x2, blocking collectives: 47.3 us -> 61.3 us  [body(): lax.all_gather(field.astype(jnp.bfloat16), 'col', axis=1, tiled=True)]
where the time goes in v1:
time: 842 us; the launch traced here: 835 us
  blocking collectives  663 us (79%)
  waiting for transfers between devices  112 us (13%)
  other arithmetic  22.3 us (3%)
  between operations  14.3 us (2%)
  matrix products  13.4 us (2%)
  local copies, waits for them, and re-layouts  10.1 us (1%)
    psum x10, blocking collectives, reduce_small(): return lax.psum(lax.psum(terms, 'col'), 'row')  557 us
    unnamed x4, waiting for transfers between devices  112 us
    all_gather x2, blocking collectives, body(): lax.all_gather(field.astype(jnp.bfloat16), 'col', axis=1, tiled=True)  61.3 us
    all_gather x1, blocking collectives, body(): sources = lax.all_gather(geom, 'col', axis=1, tiled=True)  25.1 us
    all_gather x1, blocking collectives, body(): targets = lax.all_gather(centroids, 'row', axis=1, tiled=True)  19.1 us
  transfers between devices with their start and end apart: 2, of which 2 were waited for; matrix products, arithmetic and copies ran while one was open for 0% of the time, Pallas kernels for 0%

profile of v1, /device:TPU:1, one launch (start us, length us, event | category | flops | bytes accessed | tf_op | source)
XLA Modules:
  0.0 835.3 jit_solution(14596988230392864560)
XLA Ops:
  8.0 69.9 %psum.84 = f32[16,16]{0,1:T(8,128)S(1)} all-reduce(f32[16,16]{0,1:T(8,128)S(1)} %fusion.59), channel_id=1, replica_groups=mesh['row'=16,'col'=32] {'col'}, use_global_device_ids=true, to_apply=%region_0.0 | all-reduce | flops 256 | bytes 2048 | tf_op jit(solution)/shard_map/psum | solution.py:27
  77.9 24.7 %psum.85 = f32[16,16]{0,1:T(8,128)S(1)} all-reduce(f32[16,16]{0,1:T(8,128)S(1)} %psum.84), channel_id=1, replica_groups=mesh['row'=16,'col'=32] {'row'}, use_global_device_ids=true, to_apply=%region_1.0 | all-reduce | flops 256 | bytes 2048 | tf_op jit(solution)/shard_map/psum | solution.py:27
  102.6 1.5 cholesky.94
  107.0 32.9 %all-gather = bf16[32,64,16]{1,2,0:T(8,128)(2,1)S(1)} all-gather(bf16[1,64,16]{1,2,0:T(8,128)(2,1)S(1)} %convert_bitcast_fusion.1), channel_id=1, replica_groups=mesh['row'=16,'col'=32] {'col'}, dimensions={0}, use_global_device_ids=true | all-gather | bytes 67584 | tf_op jit(solution)/shard_map/all_gather | solution.py:48
  140.2 25.1 %all-gather.1 = f32[32,64,4]{1,2,0:T(4,128)S(1)} all-gather(f32[1,64,4]{1,2,0:T(4,128)S(1)} %maximum_bitcast_fusion), channel_id=1, replica_groups=mesh['row'=16,'col'=32] {'col'}, dimensions={0}, use_global_device_ids=true | all-gather | bytes 33792 | tf_op jit(solution)/shard_map/all_gather | solution.py:38
  165.4 19.1 %all-gather.2 = f32[16,64,3]{1,2,0:T(4,128)S(1)} all-gather(f32[1,64,3]{1,2,0:T(4,128)S(1)} %bitcast.175), channel_id=1, replica_groups=mesh['row'=16,'col'=32] {'row'}, dimensions={0}, use_global_device_ids=true | all-gather | bytes 13056 | tf_op jit(solution)/shard_map/all_gather | solution.py:39
  184.6 4.5 while.34
  190.2 58.7 %reduce-scatter.7.cloned.1.call-done = f32[64,16]{1,0:T(8,128)} async-done(((f32[1024,16]{1,0:T(8,128)}), f32[64,16]{1,0:T(8,128)}) %reduce-scatter.7.cloned.1.call-update) | async-done | bytes 4112
  249.8 74.7 %psum.86 = f32[16,16]{1,0:T(8,128)S(1)} all-reduce(f32[16,16]{1,0:T(8,128)S(1)} %fusion.46), channel_id=1, replica_groups=mesh['row'=16,'col'=32] {'col'}, use_global_device_ids=true, to_apply=%region_7.0 | all-reduce | flops 256 | bytes 2048 | tf_op jit(solution)/shard_map/psum | solution.py:27
  324.5 22.0 %psum.87 = f32[16,16]{1,0:T(8,128)S(1)} all-reduce(f32[16,16]{1,0:T(8,128)S(1)} %psum.86), channel_id=1, replica_groups=mesh['row'=16,'col'=32] {'row'}, use_global_device_ids=true, to_apply=%region_8.0 | all-reduce | flops 256 | bytes 2048 | tf_op jit(solution)/shard_map/psum | solution.py:27
  346.8 70.7 %psum.88 = f32[16,16]{0,1:T(8,128)S(1)} all-reduce(f32[16,16]{0,1:T(8,128)S(1)} %fusion.61), channel_id=1, replica_groups=mesh['row'=16,'col'=32] {'col'}, use_global_device_ids=true, to_apply=%region_9.0 | all-reduce | flops 256 | bytes 2048 | tf_op jit(solution)/shard_map/psum | solution.py:27
  417.5 22.2 %psum.89 = f32[16,16]{0,1:T(8,128)S(1)} all-reduce(f32[16,16]{0,1:T(8,128)S(1)} %psum.88), channel_id=1, replica_groups=mesh['row'=16,'col'=32] {'row'}, use_global_device_ids=true, to_apply=%region_10.0 | all-reduce | flops 256 | bytes 2048 | tf_op jit(solution)/shard_map/psum | solution.py:27
  439.8 1.5 cholesky.105
  444.2 28.4 %all-gather.3 = bf16[32,64,16]{1,2,0:T(8,128)(2,1)S(1)} all-gather(bf16[1,64,16]{1,2,0:T(8,128)(2,1)S(1)} %convert_bitcast_fusion), channel_id=1, replica_groups=mesh['row'=16,'col'=32] {'col'}, dimensions={0}, use_global_device_ids=true | all-gather | bytes 67584 | tf_op jit(solution)/shard_map/all_gather | solution.py:48
  472.8 4.5 while.35
  480.2 53.5 %reduce-scatter.9.cloned.1.call-done = f32[64,16]{1,0:T(8,128)} async-done(((f32[1024,16]{1,0:T(8,128)}), f32[64,16]{1,0:T(8,128)}) %reduce-scatter.9.cloned.1.call-update) | async-done | bytes 4112
  534.8 129.5 %all-reduce.2 = (f32[16,16]{1,0:T(8,128)S(1)}, f32[16,16]{1,0:T(8,128)S(1)}) all-reduce(f32[16,16]{1,0:T(8,128)S(1)} %fusion.54, f32[16,16]{1,0:T(8,128)S(1)} %fusion.53), channel_id=1, replica_groups=mesh['row'=16,'col'=32] {'col'}, use_global_device_ids=true, to_apply=%region_15.0 | all-reduce | flops 512 | bytes 4096 | tf_op jit(solution)/shard_map/psum | solution.py:27
  664.3 40.4 %all-reduce.3 = (f32[16,16]{1,0:T(8,128)S(1)}, f32[16,16]{1,0:T(8,128)S(1)}) all-reduce(f32[16,16]{1,0:T(8,128)S(1)} %get-tuple-element.322, f32[16,16]{1,0:T(8,128)S(1)} %get-tuple-element.323), channel_id=1, replica_groups=mesh['row'=16,'col'=32] {'row'}, use_global_device_ids=true, to_apply=%region_16.0 | all-reduce | flops 512 | bytes 4096 | tf_op jit(solution)/shard_map/psum | solution.py:27
  705.2 82.1 %psum.94 = f32[16,16]{0,1:T(8,128)S(1)} all-reduce(f32[16,16]{0,1:T(8,128)S(1)} %fusion.63), channel_id=1, replica_groups=mesh['row'=16,'col'=32] {'col'}, use_global_device_ids=true, to_apply=%region_19.0 | all-reduce | flops 256 | bytes 2048 | tf_op jit(solution)/shard_map/psum | solution.py:27
  787.3 21.1 %psum.95 = f32[16,16]{0,1:T(8,128)S(1)} all-reduce(f32[16,16]{0,1:T(8,128)S(1)} %psum.94), channel_id=1, replica_groups=mesh['row'=16,'col'=32] {'row'}, use_global_device_ids=true, to_apply=%region_20.0 | all-reduce | flops 256 | bytes 2048 | tf_op jit(solution)/shard_map/psum | solution.py:27
  811.5 2.0 dynamic-slice_select_fusion
  813.5 2.1 scatter.24
  817.5 2.9 cholesky.41
  821.7 2.4 custom-call.15
  (113 shorter events, 33.6 us)
Async XLA Ops:
  7.2 0.7 copy-start
  7.2 133.0 %copy-start.3 = (f32[64]{0:T(128)S(1)}, f32[64]{0:T(128)}, u32[]{:S(2)}) copy-start(f32[64]{0:T(128)} %param.24) | copy-start | bytes 772
  7.2 133.0 %copy-start.2 = (f32[3,64]{1,0:T(4,128)S(1)}, f32[3,64]{1,0:T(4,128)}, u32[]{:S(2)}) copy-start(f32[3,64]{1,0:T(4,128)} %param.23) | copy-start | bytes 2308
  7.2 241.7 %reduce-scatter.7.cloned.1.call-start = ((), (), s32[]{:S(2)}) async-start(), calls=%async_computation.2 | async-start | bytes 557056
  189.1 60.6 %copy-start.1 = (f32[64]{0:T(128)S(1)}, f32[64]{0:T(128)}, u32[]{:S(2)}) copy-start(f32[64]{0:T(128)} %param.25) | copy-start | bytes 772
  190.1 343.6 %reduce-scatter.9.cloned.1.call-start = ((), (), s32[]{:S(2)}) async-start(), calls=%async_computation.3 | async-start | bytes 557056
  477.3 1.6 copy-start.4
Sparse Core Ops, SparseCore 0:
  190.2 58.5 reduce-scatter.6
  478.5 55.1 reduce-scatter.8
